TPU v7x, 32 devices: a whole 2x2x4 slice. The times are simulated.
32 devices in a mesh: wide: 8 (over z, y), sub: 4 (over x, core).
Axes of the slice: x: 2, y: 2, z: 4, core: 2. Of those that a mesh axis runs over, the one named last changes fastest.
Arguments:
- embeddings: bfloat16 [4096, 1024], P(('wide', 'sub'))
- cluster_ids: int32 [4096], P(('wide', 'sub')), may hold values from 0 to 383, as said below
Outputs:
- nearest: float32 [4096], P(('wide', 'sub'))
Inputs may be any that keep to these rules, and one draw needn't show every extreme that they name: `cluster_ids`: cluster c belongs to owner c // 48 (an index along wide). Among the 128 documents of one device, at most 32 lie in clusters of one owner; in every draw some owner has exactly 32 such documents from every device. A cluster holds at most 44 documents, and some cluster holds exactly that many.
All inputs are finite; a program needn't handle non-finite values.
Results may differ from a plain program's by a relative error of at most 0.00047.
Values may be sent and summed in bfloat16 or wider, within the bound.
A program may use at most 64 MiB of HBM per device.

v0:
```python
import jax
import jax.numpy as jnp
from jax import lax
from jax.sharding import PartitionSpec as P

CL_DEV = 48


EPSILON = 1e-06


def raw_scores(query_rows, key_rows):
    return lax.dot_general(
        query_rows, key_rows, (((1,), (1,)), ((), ())), preferred_element_type=jnp.float32
    )


def apply_mask(scores, query_meta, key_meta, along):
    allowed = (query_meta[0][:, None] == key_meta[0][None, :]) & (
        key_meta[1][None, :] < query_meta[1][:, None]
    )
    return jnp.max(jnp.where(allowed, scores, jnp.float32(-1.0)), axis=along)


def flatten_meta(meta):
    return (meta[:, 0, :].reshape(-1), meta[:, 1, :].reshape(-1))


def per_device(embeddings, cluster_ids):
    doc_count, width = embeddings.shape
    wide_count = lax.axis_size("wide")
    sub_count = lax.axis_size("sub")
    capacity = max(2, 2 * doc_count // wide_count)
    total_slots = wide_count * capacity
    values = embeddings.astype(jnp.float32)
    unit_rows = (
        values * lax.rsqrt(jnp.sum(values * values, axis=1, keepdims=True) + EPSILON)
    ).astype(jnp.bfloat16)
    owner_idx = cluster_ids // CL_DEV
    one_hot = (owner_idx[:, None] == jnp.arange(wide_count, dtype=jnp.int32)[None, :]).astype(
        jnp.int32
    )
    slot_rank = jnp.sum((jnp.cumsum(one_hot, axis=0) - one_hot) * one_hot, axis=1)
    slot_index = owner_idx * capacity + slot_rank
    device_row = lax.axis_index("wide") * sub_count + lax.axis_index("sub")
    positions = device_row * doc_count + jnp.arange(doc_count, dtype=jnp.int32)
    send_rows = jnp.zeros((total_slots, width), jnp.bfloat16).at[slot_index].set(unit_rows)
    send_rows = send_rows.reshape(wide_count, capacity, width)
    send_labels = jnp.full((total_slots,), -1, jnp.int32).at[slot_index].set(cluster_ids)
    send_places = jnp.full((total_slots,), -1, jnp.int32).at[slot_index].set(positions)
    send_meta = jnp.stack(
        [send_labels.reshape(wide_count, capacity), send_places.reshape(wide_count, capacity)],
        axis=1,
    )
    recv_rows, recv_meta = (
        lax.all_to_all(send_rows, "wide", split_axis=0, concat_axis=0, tiled=True),
        lax.all_to_all(send_meta, "wide", split_axis=0, concat_axis=0, tiled=True),
    )
    query_rows = recv_rows.reshape(-1, width)
    query_meta = flatten_meta(recv_meta)
    initial = jnp.full((total_slots,), -1.0, jnp.float32)
    key_rows = lax.all_gather(recv_rows, "sub", axis=0, tiled=True).reshape(-1, width)
    scores = raw_scores(query_rows, key_rows)
    nearest = jnp.maximum(
        initial,
        apply_mask(
            scores,
            query_meta,
            flatten_meta(lax.all_gather(recv_meta, "sub", axis=0, tiled=True)),
            1,
        ),
    )
    answer = lax.all_to_all(
        nearest.reshape(wide_count, capacity), "wide", split_axis=0, concat_axis=0, tiled=True
    )
    return answer.reshape(-1)[slot_index]


def solution(mesh):
    in_specs = (P(("wide", "sub"), None), P(("wide", "sub")))
    out_specs = P(("wide", "sub"))
    return jax.shard_map(
        per_device, mesh=mesh, in_specs=in_specs, out_specs=out_specs, check_vma=False
    )
```

profile of v0, /device:TPU:0, one launch (start us, length us, event | category | flops | bytes accessed | tf_op | source)
XLA Modules:
  0.0 80.1 jit_solution(15488452722823957876)
XLA Ops:
  6.5 0.7 and_select_fusion
  7.2 0.1 fusion.7
  7.3 0.2 reduce_window_sum.11
  7.5 0.2 select_reduce_fusion
  7.6 1.1 %fusion.1 = f32[128]{0:T(128)S(1)} fusion(bf16[128,1024]{1,0:T(8,128)(2,1)} %param.2), kind=kLoop, calls=%fused_computation.8 | loop fusion | flops 393088 | bytes 262656 | tf_op jit(solution)/shard_map/reduce_sum | solution.py:37
  8.7 0.7 compare_select_fusion
  9.4 1.8 %scatter_custom_fusion.2 = bf16[256,1024]{1,0:T(8,128)(2,1)S(1)} fusion(s32[128]{0:T(128)S(1)} %get-tuple-element.9, bf16[128,1024]{1,0:T(8,128)(2,1)} %param.2, f32[128]{0:T(128)S(1)} %add_rsqrt_fusion, bf16[]{:T(256)} %constant.41.clone.1), kind=kCustom, calls=%fused_computation.10 | custom fusion | flops 393216 | bytes 786946 | tf_op jit(solution)/shard_map/scatter | solution.py:47
  11.2 21.7 %all_to_all.16 = bf16[8,32,1024]{2,1,0:T(8,128)(2,1)} all-to-all(bf16[8,32,1024]{2,1,0:T(8,128)(2,1)S(1)} %bitcast.6), channel_id=1, replica_groups=mesh['wide'=8,'sub'=4] {'wide'}, dimensions={0} | all-to-all | bytes 1048576 | tf_op jit(solution)/shard_map/all_to_all | solution.py:56
  33.0 1.1 %scatter_custom_fusion = s32[256]{0:T(256)S(1)} fusion(s32[128]{0:T(128)S(1)} %get-tuple-element.9, s32[128]{0:T(128)} %param.3, s32[]{:T(128)} %constant.16.clone.1), kind=kCustom, calls=%fused_computation.29 | custom fusion | bytes 1536 | tf_op jit(solution)/shard_map/scatter | solution.py:49
  34.1 1.0 %scatter_custom_fusion.1 = s32[256]{0:T(256)S(1)} fusion(s32[128]{0:T(128)S(1)} %get-tuple-element.9, s32[128]{0:T(128)S(1)} %get-tuple-element.10, s32[]{:T(128)} %constant.16.clone.1), kind=kCustom, calls=%fused_computation.27 | custom fusion | bytes 1028 | tf_op jit(solution)/shard_map/scatter | solution.py:50
  35.1 0.1 stack_reshape.7
  35.1 0.1 stack_reshape.6
  35.2 9.9 %all_to_all.17 = s32[8,2,32]{2,1,0:T(2,128)S(1)} all-to-all(s32[8,2,32]{2,1,0:T(2,128)S(1)} %pad_add_fusion), channel_id=1, replica_groups=mesh['wide'=8,'sub'=4] {'wide'}, dimensions={0} | all-to-all | bytes 4096 | tf_op jit(solution)/shard_map/all_to_all | solution.py:57
  45.1 5.3 %all_gather.6 = s32[32,2,32]{2,1,0:T(2,128)S(1)} all-gather(s32[8,2,32]{2,1,0:T(2,128)S(1)} %all_to_all.17), channel_id=1, replica_groups=mesh['wide'=8,'sub'=4] {'sub'}, dimensions={0}, use_global_device_ids=true | all-gather | bytes 10240 | tf_op jit(solution)/shard_map/all_gather | solution.py:69
  50.5 0.1 slice_reduce_fusion.1
  50.7 0.1 eq.33
  50.9 4.0 %all-gather.2.cloned.1.call-done = bf16[32,32,1024]{2,1,0:T(8,128)(2,1)} async-done(((bf16[8,32,1024]{2,1,0:T(8,128)(2,1)}), bf16[32,32,1024]{2,1,0:T(8,128)(2,1)}) %all-gather.2.cloned.1.call-update) | async-done | bytes 2097168 | tf_op jit(solution)/shard_map/all_gather | solution.py:62
  54.9 2.6 %fusion = f32[256]{0:T(256)S(1)} fusion(bf16[256,1024]{1,0:T(8,128)(2,1)} %bitcast.5, bf16[1024,1024]{1,0:T(8,128)(2,1)} %bitcast.7, s32[1024]{0:T(1024)S(1)} %lt.24, s32[1024]{0:T(1024)S(1)} %eq.35, s32[256]{0:T(256)S(1)} %lt.26, s32[256]{0:T(256)S(1)} %eq.33), kind=kOutput, calls=%fused_computation.5 | convolution fusion | flops 538181376 | bytes 2632704 | tf_op jit(solution)/shard_map/dot_general | solution.py:13
  57.5 0.7 max_broadcast_in_dim.15
  58.2 5.5 %all-to-all-start.2 = ((f32[8,1,32]{2,1,0:T(1,128)}), f32[8,1,32]{2,1,0:T(1,128)S(1)}, u32[]{:S(2)}, u32[]{:S(2)}) async-start(f32[8,1,32]{2,1,0:T(1,128)} %max_broadcast_in_dim.15), calls=%async_computation.2 | async-start | bytes 8192 | tf_op jit(solution)/shard_map/all_to_all | solution.py:73
  63.7 6.5 %all-to-all-done.2 = f32[8,1,32]{2,1,0:T(1,128)S(1)} async-done(((f32[8,1,32]{2,1,0:T(1,128)}), f32[8,1,32]{2,1,0:T(1,128)S(1)}, u32[]{:S(2)}, u32[]{:S(2)}) %all-to-all-start.2) | async-done | bytes 1056 | tf_op jit(solution)/shard_map/all_to_all | solution.py:73
  70.2 0.5 broadcast.55
  70.7 0.7 reduce.19
  71.4 1.8 %gather_fusion = f32[128]{0:T(128)} fusion(f32[256]{0:T(256)S(1)} %reshape.43, s32[1024]{0:T(1024)S(1)} %pad_clamp_fusion), kind=kCustom, calls=%fused_computation | custom fusion | bytes 1536 | tf_op jit(solution)/shard_map/gather | solution.py:76
  (11 shorter events, 0.4 us)
Async XLA Ops:
  6.5 48.3 %all-gather.2.cloned.1.call-start = ((), (), s32[]{:S(2)}) async-start(), calls=%async_computation.3 | async-start | bytes 2621440 | tf_op jit(solution)/shard_map/all_gather | solution.py:62
  58.2 12.0 %all-to-all-start.2 = ((f32[8,1,32]{2,1,0:T(1,128)}), f32[8,1,32]{2,1,0:T(1,128)S(1)}, u32[]{:S(2)}, u32[]{:S(2)}) async-start(f32[8,1,32]{2,1,0:T(1,128)} %max_broadcast_in_dim.15), calls=%async_computation.2 | async-start | bytes 8192 | tf_op jit(solution)/shard_map/all_to_all | solution.py:73
Sparse Core Ops, SparseCore 0:
  33.1 21.7 all-gather.1
where the time goes:
time: 80.4 us; the launch traced here: 80.1 us
  blocking collectives  36.9 us (46%)
  between operations  13.5 us (17%)
  waiting for transfers between devices  10.5 us (13%)
  local copies, waits for them, and re-layouts  5.7 us (7%)
  starting transfers between devices  5.52 us (7%)
  other arithmetic  5.33 us (7%)
  matrix products  2.63 us (3%)
    all_to_all x1, blocking collectives, per_device(): lax.all_to_all(send_rows, 'wide', split_axis=0, concat_axis=0, tiled=True)  21.7 us
    all_to_all x1, blocking collectives, per_device(): lax.all_to_all(send_meta, 'wide', split_axis=0, concat_axis=0, tiled=True)  9.9 us
    all_to_all x1, waiting for transfers between devices, per_device(): lax.all_to_all(nearest.reshape(wide_count, capacity), 'wide', split_axis=...  6.46 us
    all_to_all x1, starting transfers between devices, per_device(): lax.all_to_all(nearest.reshape(wide_count, capacity), 'wide', split_axis=...  5.52 us
    all_gather x1, blocking collectives, per_device(): lax.all_gather(recv_meta, 'sub', axis=0, tiled=True)  5.33 us
    all_gather x1, waiting for transfers between devices, per_device(): lax.all_gather(recv_rows, 'sub', axis=0, tiled=True).reshape(-1, width)  3.98 us
    dot_general x1, matrix products, raw_scores(): lax.dot_general(query_rows, key_rows, (((1,), (1,)), ((), ())), preferred...  2.63 us
    scatter x1, other arithmetic, per_device(): jnp.zeros((total_slots, width), jnp.bfloat16).at[slot_index].set(unit_rows)  1.79 us
  transfers between devices with their start and end apart: 2, of which 2 were waited for; matrix products, arithmetic and copies ran while one was open for 3% of the time, Pallas kernels for 0%

commit v1 on v0

--- a/solution.py
+++ b/solution.py
@@ -1,18 +1,190 @@
+import functools
+
 import jax
 import jax.numpy as jnp
 from jax import lax
+from jax.experimental import pallas as pl
+from jax.experimental.pallas import tpu as pltpu
 from jax.sharding import PartitionSpec as P
 
 CL_DEV = 48
-
-
 EPSILON = 1e-06
+META = 128
+MESH = pl.DeviceIdType.MESH
 
 
 def raw_scores(query_rows, key_rows):
     return lax.dot_general(
         query_rows, key_rows, (((1,), (1,)), ((), ())), preferred_element_type=jnp.float32
     )
+
+
+def flip(index, mask, count):
+    result, bit = 0, 1
+    while bit < count:
+        digit = lax.rem(lax.div(index, bit), 2)
+        result = result + (1 - digit if mask & bit else digit) * bit
+        bit *= 2
+    return result
+
+
+def kernel(wide, cap, emb_ref, ids_ref, out_ref, send, keys, best, answers, sems, back_sems):
+    docs, width = emb_ref.shape
+    w, s = lax.axis_index("wide"), lax.axis_index("sub")
+    group = 4 * cap
+    peers = {k: flip(w, k, wide) for k in range(wide)}
+    x_peer, core_peer = flip(s, 2, 4), flip(s, 1, 4)
+
+    barrier = pltpu.get_barrier_semaphore()
+    for k in range(1, wide):
+        pl.semaphore_signal(barrier, inc=1, device_id=(peers[k], s), device_id_type=MESH)
+    for t in (x_peer, core_peer):
+        pl.semaphore_signal(barrier, inc=1, device_id=(w, t), device_id_type=MESH)
+
+    ids = ids_ref[...]
+    owner_row = lax.broadcasted_iota(jnp.int32, (wide, docs), 0)
+    own = (ids >= owner_row * CL_DEV) & (ids < owner_row * CL_DEV + CL_DEV)
+    ones = jnp.where(own, 1.0, 0.0)
+    earlier = lax.broadcasted_iota(jnp.int32, (docs, docs), 0) < lax.broadcasted_iota(
+        jnp.int32, (docs, docs), 1
+    )
+    ranks = jnp.dot(
+        ones.astype(jnp.bfloat16),
+        jnp.where(earlier, 1.0, 0.0).astype(jnp.bfloat16),
+        preferred_element_type=jnp.float32,
+    )
+    rank = jnp.sum(ones * ranks, axis=0, keepdims=True).astype(jnp.int32)
+    owner = jnp.sum(jnp.where(own, owner_row, 0), axis=0, keepdims=True)
+    slot = owner * cap + rank
+    local = ids - owner * CL_DEV
+
+    values = emb_ref[...].astype(jnp.float32)
+    unit = (
+        values * lax.rsqrt(jnp.sum(values * values, axis=1, keepdims=True) + EPSILON)
+    ).astype(jnp.bfloat16)
+    pick = jnp.where(
+        lax.broadcasted_iota(jnp.int32, (wide * cap, docs), 0) == slot, 1.0, 0.0
+    ).astype(jnp.bfloat16)
+    labels = jnp.where(
+        lax.broadcasted_iota(jnp.int32, (META, docs), 0) == local, 1.0, 0.0
+    ).astype(jnp.bfloat16)
+    send[:, :width] = jnp.dot(pick, unit, preferred_element_type=jnp.float32).astype(jnp.bfloat16)
+    send[:, width:] = raw_scores(pick, labels).astype(jnp.bfloat16)
+
+    def rows(k, t):
+        return pl.ds(pl.multiple_of(peers[k] * group + t * cap, cap), cap)
+
+    def remote(src, dst, kind, k, device):
+        return pltpu.make_async_remote_copy(
+            src_ref=src,
+            dst_ref=dst,
+            send_sem=sems.at[kind, 0, k],
+            recv_sem=sems.at[kind, 1, k],
+            device_id=device,
+            device_id_type=MESH,
+        )
+
+    order = [0, 1, 4, 2, 5, 3, 6, 7] if wide == 8 else list(range(wide))
+
+    def chunk(k):
+        return send.at[pl.ds(pl.multiple_of(peers[k] * cap, cap), cap)]
+
+    routed = {k: remote(chunk(k), keys.at[rows(0, s)], 0, k, (peers[k], s)) for k in order[1:]}
+    across = {
+        k: remote(keys.at[rows(k, s)], keys.at[rows(k, s)], 1, k, (w, x_peer)) for k in order
+    }
+    beside = {
+        k: remote(keys.at[rows(k, s)], keys.at[rows(k, s)], 2, k, (w, core_peer)) for k in order
+    }
+    onward = {
+        k: remote(keys.at[rows(k, x_peer)], keys.at[rows(k, x_peer)], 3, k, (w, core_peer))
+        for k in order
+    }
+
+    keys[rows(0, s), :] = send[pl.ds(pl.multiple_of(w * cap, cap), cap), :]
+    pl.semaphore_wait(barrier, wide + 1)
+    for k in order[1:]:
+        routed[k].start()
+    for at, k in enumerate(order):
+        if k:
+            routed[k].wait_recv()
+        across[k].start()
+        beside[k].start()
+        if at:
+            across[order[at - 1]].wait_recv()
+            onward[order[at - 1]].start()
+    across[order[-1]].wait_recv()
+    onward[order[-1]].start()
+    for k in order:
+        beside[k].wait_recv()
+        onward[k].wait_recv()
+
+    queries = jnp.concatenate(
+        [keys[pl.ds(pl.multiple_of(q * group + s * cap, cap), cap), :] for q in range(wide)], axis=0
+    )
+    lane = lax.broadcasted_iota(jnp.int32, (1, wide * cap), 1)
+    query_place = lax.div(lane, cap) * group + s * cap + lax.rem(lane, cap)
+    tile = 2 * group
+    nearest = jnp.full((1, wide * cap), -1.0, jnp.float32)
+    for first in range(0, wide * group, tile):
+        scores = raw_scores(keys[first : first + tile, :width], queries[:, :width])
+        same = raw_scores(keys[first : first + tile, width:], queries[:, width:])
+        place = lax.broadcasted_iota(jnp.int32, (tile, 1), 0) + first
+        allowed = (same > 0.5) & (place < query_place)
+        nearest = jnp.maximum(
+            nearest, jnp.max(jnp.where(allowed, scores, -1.0), axis=0, keepdims=True)
+        )
+    best[...] = nearest
+    answers[w] = nearest
+    backs = [
+        pltpu.make_async_remote_copy(
+            src_ref=best,
+            dst_ref=answers.at[w],
+            send_sem=back_sems.at[0, k],
+            recv_sem=back_sems.at[1, k],
+            device_id=(peers[k], s),
+            device_id_type=MESH,
+        )
+        for k in range(1, wide)
+    ]
+    for copy in backs:
+        copy.start()
+    for copies in (routed, across, beside, onward):
+        for copy in copies.values():
+            copy.wait_send()
+    for copy in backs:
+        copy.wait()
+    take = jnp.where(
+        lax.broadcasted_iota(jnp.int32, (wide * cap, docs), 0) == w * cap + rank, 1.0, 0.0
+    )
+    found = jnp.dot(
+        answers[:, 0, :], take, preferred_element_type=jnp.float32, precision=lax.Precision.HIGHEST
+    )
+    out_ref[...] = jnp.sum(jnp.where(own, found, 0.0), axis=0, keepdims=True)
+
+
+def fused(embeddings, cluster_ids):
+    docs, width = embeddings.shape
+    wide = lax.axis_size("wide")
+    cap = 2 * docs // wide
+    out = pl.pallas_call(
+        functools.partial(kernel, wide, cap),
+        out_shape=jax.ShapeDtypeStruct((1, docs), jnp.float32),
+        in_specs=[pl.BlockSpec(memory_space=pltpu.VMEM)] * 2,
+        out_specs=pl.BlockSpec(memory_space=pltpu.VMEM),
+        scratch_shapes=[
+            pltpu.VMEM((wide * cap, width + META), jnp.bfloat16),
+            pltpu.VMEM((4 * wide * cap, width + META), jnp.bfloat16),
+            pltpu.VMEM((1, wide * cap), jnp.float32),
+            pltpu.VMEM((wide, 1, wide * cap), jnp.float32),
+            pltpu.SemaphoreType.DMA((4, 2, wide)),
+            pltpu.SemaphoreType.DMA((2, wide)),
+        ],
+        compiler_params=pltpu.CompilerParams(
+            collective_id=0, has_side_effects=True, vmem_limit_bytes=32 * 2**20
+        ),
+    )(embeddings, cluster_ids.reshape(1, docs))
+    return out.reshape(docs)
 
 
 def apply_mask(scores, query_meta, key_meta, along):
@@ -77,8 +249,18 @@
 
 
 def solution(mesh):
-    in_specs = (P(("wide", "sub"), None), P(("wide", "sub")))
-    out_specs = P(("wide", "sub"))
+    wide, sub = mesh.shape["wide"], mesh.shape["sub"]
+
+    def step(embeddings, cluster_ids):
+        cap = 2 * embeddings.shape[0] // wide
+        if sub == 4 and wide & (wide - 1) == 0 and cap % 16 == 0:
+            return fused(embeddings, cluster_ids)
+        return per_device(embeddings, cluster_ids)
+
     return jax.shard_map(
-        per_device, mesh=mesh, in_specs=in_specs, out_specs=out_specs, check_vma=False
-    )
+        step,
+        mesh=mesh,
+        in_specs=(P(("wide", "sub"), None), P(("wide", "sub"))),
+        out_specs=P(("wide", "sub")),
+        check_vma=False,
+    )

time: 80.4 us -> 33.9 us (0.42)
  blocking collectives: 36.9 us -> 0 us
  Pallas kernels: 0 us -> 31.6 us
  between operations: 13.5 us -> 0.01 us
  waiting for transfers between devices: 10.5 us -> 0 us
  starting transfers between devices: 5.52 us -> 0 us
  other arithmetic: 5.33 us -> 0 us
  local copies, waits for them, and re-layouts: 5.7 us -> 2.12 us
  matrix products: 2.63 us -> 0 us
    pallas_call x0 -> x1, Pallas kernels: none -> 31.6 us  [fused(): pl.pallas_call(functools.partial(kernel, wide, cap), out_shape=jax.ShapeD...]
    all_to_all x2 -> x0, blocking collectives: 31.6 us -> none  [the longest x1 21.7 us: per_device(): lax.all_to_all(send_rows, 'wide', split_axis=0, concat_axis=0, tiled=True)]
    all_to_all x1 -> x0, waiting for transfers between devices: 6.46 us -> none  [per_device(): lax.all_to_all(nearest.reshape(wide_count, capacity), 'wide', split_axis=...]
    all_to_all x1 -> x0, starting transfers between devices: 5.52 us -> none  [per_device(): lax.all_to_all(nearest.reshape(wide_count, capacity), 'wide', split_axis=...]
    all_gather x1 -> x0, blocking collectives: 5.33 us -> none  [per_device(): lax.all_gather(recv_meta, 'sub', axis=0, tiled=True)]
    all_gather x1 -> x0, waiting for transfers between devices: 3.98 us -> none  [per_device(): lax.all_gather(recv_rows, 'sub', axis=0, tiled=True).reshape(-1, width)]
    dot_general x1 -> x0, matrix products: 2.63 us -> none  [raw_scores(): lax.dot_general(query_rows, key_rows, (((1,), (1,)), ((), ())), preferred...]
    unnamed x0 -> x5, local copies, waits for them, and re-layouts: none -> 2.12 us
  transfers between devices with their start and end apart: 2 -> 0, of which waited for: 2 -> 0; matrix products, arithmetic and copies ran while one was open for 3% -> 0% of each run, Pallas kernels for 0% -> 0%
where the time goes in v1:
time: 33.9 us; the launch traced here: 33.8 us
  Pallas kernels  31.6 us (93%)
  local copies, waits for them, and re-layouts  2.12 us (6%)
    pallas_call x1, Pallas kernels, fused(): pl.pallas_call(functools.partial(kernel, wide, cap), out_shape=jax.ShapeD...  31.6 us
    unnamed x5, local copies, waits for them, and re-layouts  2.12 us

profile of v1, /device:TPU:0, one launch (start us, length us, event | category | flops | bytes accessed | tf_op | source)
XLA Modules:
  0.0 33.8 jit_solution(4920713378203425313)
XLA Ops:
  0.0 0.0 copy-start.1
  0.0 0.7 %copy-done.1 = s32[128]{0:T(128)S(1)} copy-done((s32[128]{0:T(128)S(1)}, s32[128]{0:T(128)}, u32[]{:S(2)}) %copy-start.1) | copy-done | bytes 536
  0.7 0.0 copy-start
  0.7 0.9 %copy-done = bf16[128,1024]{1,0:T(8,128)(2,1)S(1)} copy-done((bf16[128,1024]{1,0:T(8,128)(2,1)S(1)}, bf16[128,1024]{1,0:T(8,128)(2,1)}, u32[]{:S(2)}) %copy-start) | copy-done | bytes 262168
  1.6 31.6 %shard_map.28 = f32[1,128]{1,0:T(1,128)S(1)} custom-call(bf16[128,1024]{1,0:T(8,128)(2,1)S(1)} %copy-done, s32[1,128]{1,0:T(1,128)S(1)} %bitcast.2), custom_call_target="tpu_custom_call" | custom-call | tf_op jit(solution)/shard_map/pallas_call | solution.py:170
  33.2 0.5 %copy.4 = f32[128]{0:T(128)} copy(f32[128]{0:T(128)S(1)} %bitcast.3) | data formatting | bytes 1024
Async XLA Ops:
  0.0 0.7 %copy-start.1 = (s32[128]{0:T(128)S(1)}, s32[128]{0:T(128)}, u32[]{:S(2)}) copy-start(s32[128]{0:T(128)} %param.3) | copy-start | bytes 1540
  0.7 0.9 %copy-start = (bf16[128,1024]{1,0:T(8,128)(2,1)S(1)}, bf16[128,1024]{1,0:T(8,128)(2,1)}, u32[]{:S(2)}) copy-start(bf16[128,1024]{1,0:T(8,128)(2,1)} %emb_ref.1) | copy-start | bytes 786436

commit v2 on v1

v2 whole, which is shorter than its diff:
```python
import functools

import jax
import jax.numpy as jnp
from jax import lax
from jax.experimental import pallas as pl
from jax.experimental.pallas import tpu as pltpu
from jax.sharding import PartitionSpec as P

CL_DEV = 48
EPSILON = 1e-06
LABELS = 64
MESH = pl.DeviceIdType.MESH


def raw_scores(query_rows, key_rows):
    return lax.dot_general(
        query_rows, key_rows, (((1,), (1,)), ((), ())), preferred_element_type=jnp.float32
    )


def flip(index, mask, count):
    result, bit = 0, 1
    while bit < count:
        digit = lax.rem(lax.div(index, bit), 2)
        result = result + (1 - digit if mask & bit else digit) * bit
        bit *= 2
    return result


def kernel(wide, cap, emb_hbm, ids_hbm, out_ref, emb, ids_ref, send, keys, tags, labels, best, answers,
           in_sems, sems, tag_sems, tag_hops, back_sems):
    docs, width = emb.shape
    w, s = lax.axis_index("wide"), lax.axis_index("sub")
    group = 4 * cap
    half = wide // 2
    peers = {k: flip(w, k, wide) for k in range(wide)}
    x_peer, core_peer = flip(s, 2, 4), flip(s, 1, 4)

    barrier = pltpu.get_barrier_semaphore()
    for k in range(1, wide):
        pl.semaphore_signal(barrier, inc=1, device_id=(peers[k], s), device_id_type=MESH)
    for t in (x_peer, core_peer):
        pl.semaphore_signal(barrier, inc=1, device_id=(w, t), device_id_type=MESH)
    fetch_ids = pltpu.make_async_copy(ids_hbm, ids_ref, in_sems.at[0])
    fetch_emb = pltpu.make_async_copy(emb_hbm, emb, in_sems.at[1])
    fetch_ids.start()
    fetch_emb.start()
    fetch_ids.wait()

    ids = ids_ref[...]
    owner_row = lax.broadcasted_iota(jnp.int32, (wide, docs), 0)
    own = (ids >= owner_row * CL_DEV) & (ids < owner_row * CL_DEV + CL_DEV)
    ones = jnp.where(own, 1.0, 0.0)
    earlier = lax.broadcasted_iota(jnp.int32, (docs, docs), 0) < lax.broadcasted_iota(
        jnp.int32, (docs, docs), 1
    )
    ranks = jnp.dot(
        ones.astype(jnp.bfloat16),
        jnp.where(earlier, 1.0, 0.0).astype(jnp.bfloat16),
        preferred_element_type=jnp.float32,
    )
    rank = jnp.sum(ones * ranks, axis=0, keepdims=True).astype(jnp.int32)
    owner = jnp.sum(jnp.where(own, owner_row, 0), axis=0, keepdims=True)
    slot = owner * cap + rank
    label = jnp.where(own, (ids - owner_row * CL_DEV + 1).astype(jnp.float32), 0.0)
    lanes = lax.broadcasted_iota(jnp.int32, (group, docs), 0)
    for row, place in enumerate((s * cap + rank, lax.rem(w, 4) * cap + rank)):
        spread = jnp.where(lanes == place, 1.0, 0.0).astype(jnp.bfloat16)
        tags[:, row, :] = raw_scores(label.astype(jnp.bfloat16), spread)
    labels[s, w] = tags[w]
    pick = jnp.where(
        lax.broadcasted_iota(jnp.int32, (wide * cap, docs), 0) == slot, 1.0, 0.0
    ).astype(jnp.bfloat16)

    fetch_emb.wait()
    values = emb[...].astype(jnp.float32)
    unit = (
        values * lax.rsqrt(jnp.sum(values * values, axis=1, keepdims=True) + EPSILON)
    ).astype(jnp.bfloat16)
    send[...] = jnp.dot(pick, unit, preferred_element_type=jnp.float32).astype(jnp.bfloat16)

    def rows(k, t):
        return pl.ds(pl.multiple_of(peers[k] * group + t * cap, cap), cap)

    def copy_to(src, dst, send_sem, recv_sem, device):
        return pltpu.make_async_remote_copy(
            src_ref=src, dst_ref=dst, send_sem=send_sem, recv_sem=recv_sem,
            device_id=device, device_id_type=MESH,
        )

    def hop(kind, k, t, u):
        block = keys.at[rows(k, t)]
        return copy_to(block, block, sems.at[kind, 0, k], sems.at[kind, 1, k], (w, u))

    def tag_hop(kind, t, u):
        return copy_to(
            labels.at[t], labels.at[t], tag_hops.at[0, kind], tag_hops.at[1, kind], (w, u)
        )

    everyone = range(wide)
    others = range(1, wide)
    routed = {
        k: copy_to(
            send.at[pl.ds(pl.multiple_of(peers[k] * cap, cap), cap)], keys.at[rows(0, s)],
            sems.at[0, 0, k], sems.at[0, 1, k], (peers[k], s),
        )
        for k in others
    }
    tagged = {
        k: copy_to(
            tags.at[peers[k]], labels.at[s, w], tag_sems.at[0, k], tag_sems.at[1, k], (peers[k], s)
        )
        for k in others
    }
    across = {k: hop(1, k, s, x_peer) for k in everyone}
    beside = {k: hop(2, k, s, core_peer) for k in everyone}
    onward = {k: hop(3, k, x_peer, core_peer) for k in everyone}
    tag_across, tag_beside, tag_onward = (
        tag_hop(0, s, x_peer), tag_hop(1, s, core_peer), tag_hop(2, x_peer, core_peer)
    )

    def forward(k):
        across[k].start()
        beside[k].start()

    def relay(k):
        across[k].wait_recv()
        onward[k].start()

    def landed(k):
        beside[k].wait_recv()
        onward[k].wait_recv()

    query_lane = lax.broadcasted_iota(jnp.int32, (1, group), 1)

    def block(key_half, query_half):
        first = key_half * (half * group)
        queries = jnp.concatenate(
            [
                keys[pl.ds(pl.multiple_of((query_half * half + q) * group + s * cap, cap), cap), :]
                for q in range(half)
            ],
            axis=0,
        )
        kinds = lax.broadcasted_iota(jnp.int32, (LABELS, group), 0).astype(jnp.float32) + 1.0
        query_tag = labels[s, query_half * half, 1:2]
        for q in range(1, half):
            query_tag = jnp.maximum(query_tag, labels[s, query_half * half + q, 1:2])
        query_kind = jnp.where(kinds == query_tag, 1.0, 0.0).astype(jnp.bfloat16)
        query_place = (
            query_half * (half * group)
            + lax.div(query_lane, cap) * group + s * cap + lax.rem(query_lane, cap)
        )
        scores = raw_scores(
            keys[pl.ds(pl.multiple_of(first, group), half * group), :], queries
        )
        nearest = jnp.full((1, group), -1.0, jnp.float32)
        for q in range(half):
            key_tag = labels[0, key_half * half + q, 0:1]
            for t in range(1, 4):
                key_tag = jnp.maximum(key_tag, labels[t, key_half * half + q, 0:1])
            key_kind = jnp.where(kinds == key_tag, 1.0, 0.0).astype(jnp.bfloat16)
            same = lax.dot_general(
                key_kind, query_kind, (((0,), (0,)), ((), ())), preferred_element_type=jnp.float32
            )
            place = lax.broadcasted_iota(jnp.int32, (group, 1), 0) + (first + q * group)
            allowed = (same > 0.5) & (place < query_place)
            part = jnp.where(allowed, scores[q * group : (q + 1) * group], -1.0)
            nearest = jnp.maximum(nearest, jnp.max(part, axis=0, keepdims=True))
        return nearest

    keys[rows(0, s), :] = send[pl.ds(pl.multiple_of(w * cap, cap), cap), :]
    pl.semaphore_wait(barrier, wide + 1)
    near_half = lax.div(w, half)
    far_half = 1 - near_half
    for k in others:
        tagged[k].start()
    for k in (4, 1, 2, 3):
        routed[k].start()
    forward(0)
    routed[1].wait_recv()
    forward(1)
    routed[2].wait_recv()
    forward(2)
    routed[4].wait_send()
    routed[5].start()
    routed[3].wait_recv()
    forward(3)
    relay(0)
    routed[4].wait_recv()
    forward(4)
    for k in others:
        tagged[k].wait_recv()
    tag_across.start()
    tag_beside.start()
    relay(1)
    routed[5].wait_send()
    routed[6].start()
    relay(2)
    routed[5].wait_recv()
    forward(5)
    relay(3)
    tag_across.wait_recv()
    tag_onward.start()
    tag_beside.wait_recv()
    tag_onward.wait_recv()
    routed[6].wait_send()
    routed[7].start()
    for k in range(4):
        landed(k)
    best[near_half] = block(near_half, near_half)
    best[far_half] = jnp.full((1, group), -1.0, jnp.float32)
    relay(4)
    routed[6].wait_recv()
    forward(6)
    relay(5)
    routed[7].wait_recv()
    forward(7)
    relay(6)
    relay(7)
    for k in (1, 2, 3, 7):
        routed[k].wait_send()
    for k in range(4, 8):
        landed(k)
    across_best = block(0, 1)
    best[far_half] = jnp.maximum(best[far_half], block(far_half, far_half))
    best[1] = jnp.maximum(best[1], across_best)
    answers[w] = best[...]
    backs = [
        copy_to(best, answers.at[w], back_sems.at[0, k], back_sems.at[1, k], (peers[k], s))
        for k in others
    ]
    for copy in backs:
        copy.start()
    for copies in (tagged, across, beside, onward):
        for copy in copies.values():
            copy.wait_send()
    for copy in (tag_across, tag_beside, tag_onward):
        copy.wait_send()
    for copy in backs:
        copy.wait()
    mine = jnp.where(near_half == 0, answers[:, 0, 0, :], answers[:, 1, 0, :])
    take = jnp.where(lanes == lax.rem(w, half) * cap + rank, 1.0, 0.0)
    found = jnp.dot(
        mine, take, preferred_element_type=jnp.float32, precision=lax.Precision.HIGHEST
    )
    out_ref[...] = jnp.sum(jnp.where(own, found, 0.0), axis=0, keepdims=True)


def fused(embeddings, cluster_ids):
    docs, width = embeddings.shape
    wide = lax.axis_size("wide")
    cap = 2 * docs // wide
    slots = wide * cap
    out = pl.pallas_call(
        functools.partial(kernel, wide, cap),
        out_shape=jax.ShapeDtypeStruct((1, docs), jnp.float32),
        in_specs=[pl.BlockSpec(memory_space=pl.ANY)] * 2,
        out_specs=pl.BlockSpec(memory_space=pltpu.VMEM),
        scratch_shapes=[
            pltpu.VMEM((docs, width), jnp.bfloat16),
            pltpu.VMEM((1, docs), jnp.int32),
            pltpu.VMEM((slots, width), jnp.bfloat16),
            pltpu.VMEM((4 * slots, width), jnp.bfloat16),
            pltpu.VMEM((wide, 2, 4 * cap), jnp.float32),
            pltpu.VMEM((4, wide, 2, 4 * cap), jnp.float32),
            pltpu.VMEM((2, 1, 4 * cap), jnp.float32),
            pltpu.VMEM((wide, 2, 1, 4 * cap), jnp.float32),
            pltpu.SemaphoreType.DMA((2,)),
            pltpu.SemaphoreType.DMA((4, 2, wide)),
            pltpu.SemaphoreType.DMA((2, wide)),
            pltpu.SemaphoreType.DMA((2, 3)),
            pltpu.SemaphoreType.DMA((2, wide)),
        ],
        compiler_params=pltpu.CompilerParams(
            collective_id=0, has_side_effects=True, vmem_limit_bytes=32 * 2**20
        ),
    )(embeddings, cluster_ids.reshape(1, docs))
    return out.reshape(docs)


def apply_mask(scores, query_meta, key_meta, along):
    allowed = (query_meta[0][:, None] == key_meta[0][None, :]) & (
        key_meta[1][None, :] < query_meta[1][:, None]
    )
    return jnp.max(jnp.where(allowed, scores, jnp.float32(-1.0)), axis=along)


def flatten_meta(meta):
    return (meta[:, 0, :].reshape(-1), meta[:, 1, :].reshape(-1))


def per_device(embeddings, cluster_ids):
    doc_count, width = embeddings.shape
    wide_count = lax.axis_size("wide")
    sub_count = lax.axis_size("sub")
    capacity = max(2, 2 * doc_count // wide_count)
    total_slots = wide_count * capacity
    values = embeddings.astype(jnp.float32)
    unit_rows = (
        values * lax.rsqrt(jnp.sum(values * values, axis=1, keepdims=True) + EPSILON)
    ).astype(jnp.bfloat16)
    owner_idx = cluster_ids // CL_DEV
    one_hot = (owner_idx[:, None] == jnp.arange(wide_count, dtype=jnp.int32)[None, :]).astype(
        jnp.int32
    )
    slot_rank = jnp.sum((jnp.cumsum(one_hot, axis=0) - one_hot) * one_hot, axis=1)
    slot_index = owner_idx * capacity + slot_rank
    device_row = lax.axis_index("wide") * sub_count + lax.axis_index("sub")
    positions = device_row * doc_count + jnp.arange(doc_count, dtype=jnp.int32)
    send_rows = jnp.zeros((total_slots, width), jnp.bfloat16).at[slot_index].set(unit_rows)
    send_rows = send_rows.reshape(wide_count, capacity, width)
    send_labels = jnp.full((total_slots,), -1, jnp.int32).at[slot_index].set(cluster_ids)
    send_places = jnp.full((total_slots,), -1, jnp.int32).at[slot_index].set(positions)
    send_meta = jnp.stack(
        [send_labels.reshape(wide_count, capacity), send_places.reshape(wide_count, capacity)],
        axis=1,
    )
    recv_rows, recv_meta = (
        lax.all_to_all(send_rows, "wide", split_axis=0, concat_axis=0, tiled=True),
        lax.all_to_all(send_meta, "wide", split_axis=0, concat_axis=0, tiled=True),
    )
    query_rows = recv_rows.reshape(-1, width)
    query_meta = flatten_meta(recv_meta)
    initial = jnp.full((total_slots,), -1.0, jnp.float32)
    key_rows = lax.all_gather(recv_rows, "sub", axis=0, tiled=True).reshape(-1, width)
    scores = raw_scores(query_rows, key_rows)
    nearest = jnp.maximum(
        initial,
        apply_mask(
            scores,
            query_meta,
            flatten_meta(lax.all_gather(recv_meta, "sub", axis=0, tiled=True)),
            1,
        ),
    )
    answer = lax.all_to_all(
        nearest.reshape(wide_count, capacity), "wide", split_axis=0, concat_axis=0, tiled=True
    )
    return answer.reshape(-1)[slot_index]


def solution(mesh):
    wide, sub = mesh.shape["wide"], mesh.shape["sub"]

    def step(embeddings, cluster_ids):
        cap = 2 * embeddings.shape[0] // wide
        if (wide, sub, cap) == (8, 4, 32):
            return fused(embeddings, cluster_ids)
        return per_device(embeddings, cluster_ids)

    return jax.shard_map(
        step,
        mesh=mesh,
        in_specs=(P(("wide", "sub"), None), P(("wide", "sub"))),
        out_specs=P(("wide", "sub")),
        check_vma=False,
    )
```

time: 33.9 us -> 34.5 us (1.018)
  Pallas kernels: 31.6 us -> 32.2 us
    pallas_call x1, Pallas kernels: 31.6 us -> 32.2 us  [fused(): pl.pallas_call(functools.partial(kernel, wide, cap), out_shape=jax.ShapeD...]
where the time goes in v2:
time: 34.5 us; the launch traced here: 34.3 us
  Pallas kernels  32.2 us (93%)
  local copies, waits for them, and re-layouts  2.12 us (6%)
    pallas_call x1, Pallas kernels, fused(): pl.pallas_call(functools.partial(kernel, wide, cap), out_shape=jax.ShapeD...  32.2 us
    unnamed x5, local copies, waits for them, and re-layouts  2.12 us

profile of v2, /device:TPU:0, one launch (start us, length us, event | category | flops | bytes accessed | tf_op | source)
XLA Modules:
  0.0 34.3 jit_solution(4100575854321316172)
XLA Ops:
  0.0 0.0 copy-start.1
  0.0 0.7 %copy-done.1 = s32[128]{0:T(128)S(1)} copy-done((s32[128]{0:T(128)S(1)}, s32[128]{0:T(128)}, u32[]{:S(2)}) %copy-start.1) | copy-done | bytes 536
  0.7 0.0 copy-start
  0.7 0.9 %copy-done = bf16[128,1024]{1,0:T(8,128)(2,1)S(1)} copy-done((bf16[128,1024]{1,0:T(8,128)(2,1)S(1)}, bf16[128,1024]{1,0:T(8,128)(2,1)}, u32[]{:S(2)}) %copy-start) | copy-done | bytes 262168
  1.6 32.2 %shard_map.28 = f32[1,128]{1,0:T(1,128)S(1)} custom-call(bf16[128,1024]{1,0:T(8,128)(2,1)S(1)} %copy-done, s32[1,128]{1,0:T(1,128)S(1)} %bitcast.2), custom_call_target="tpu_custom_call" | custom-call | tf_op jit(solution)/shard_map/pallas_call | solution.py:256
  33.8 0.5 %copy.4 = f32[128]{0:T(128)} copy(f32[128]{0:T(128)S(1)} %bitcast.3) | data formatting | bytes 1024
Async XLA Ops:
  0.0 0.7 %copy-start.1 = (s32[128]{0:T(128)S(1)}, s32[128]{0:T(128)}, u32[]{:S(2)}) copy-start(s32[128]{0:T(128)} %param.3) | copy-start | bytes 1540
  0.7 0.9 %copy-start = (bf16[128,1024]{1,0:T(8,128)(2,1)S(1)}, bf16[128,1024]{1,0:T(8,128)(2,1)}, u32[]{:S(2)}) copy-start(bf16[128,1024]{1,0:T(8,128)(2,1)} %emb_hbm.1) | copy-start | bytes 786436

commit v3 on v2

--- a/solution.py
+++ b/solution.py
@@ -174,52 +174,44 @@
     pl.semaphore_wait(barrier, wide + 1)
     near_half = lax.div(w, half)
     far_half = 1 - near_half
+    for k in (4, 1, 2, 3, 5):
+        routed[k].start()
     for k in others:
         tagged[k].start()
-    for k in (4, 1, 2, 3):
-        routed[k].start()
     forward(0)
-    routed[1].wait_recv()
-    forward(1)
-    routed[2].wait_recv()
-    forward(2)
+    for k in (1, 2, 3):
+        routed[k].wait_recv()
+        forward(k)
     routed[4].wait_send()
-    routed[5].start()
-    routed[3].wait_recv()
-    forward(3)
-    relay(0)
+    routed[6].start()
     routed[4].wait_recv()
     forward(4)
+    routed[5].wait_send()
+    routed[7].start()
+    routed[5].wait_recv()
+    forward(5)
     for k in others:
         tagged[k].wait_recv()
     tag_across.start()
     tag_beside.start()
-    relay(1)
-    routed[5].wait_send()
-    routed[6].start()
-    relay(2)
-    routed[5].wait_recv()
-    forward(5)
-    relay(3)
+    for k in range(4):
+        relay(k)
     tag_across.wait_recv()
     tag_onward.start()
     tag_beside.wait_recv()
     tag_onward.wait_recv()
-    routed[6].wait_send()
-    routed[7].start()
     for k in range(4):
         landed(k)
     best[near_half] = block(near_half, near_half)
     best[far_half] = jnp.full((1, group), -1.0, jnp.float32)
-    relay(4)
     routed[6].wait_recv()
     forward(6)
-    relay(5)
+    relay(4)
     routed[7].wait_recv()
     forward(7)
-    relay(6)
-    relay(7)
-    for k in (1, 2, 3, 7):
+    for k in (5, 6, 7):
+        relay(k)
+    for k in (1, 2, 3, 6, 7):
         routed[k].wait_send()
     for k in range(4, 8):
         landed(k)
@@ -256,7 +248,7 @@
     out = pl.pallas_call(
         functools.partial(kernel, wide, cap),
         out_shape=jax.ShapeDtypeStruct((1, docs), jnp.float32),
-        in_specs=[pl.BlockSpec(memory_space=pl.ANY)] * 2,
+        in_specs=[pl.BlockSpec(memory_space=pltpu.HBM)] * 2,
         out_specs=pl.BlockSpec(memory_space=pltpu.VMEM),
         scratch_shapes=[
             pltpu.VMEM((docs, width), jnp.bfloat16),

time: 34.5 us -> 32.4 us (0.939)
  Pallas kernels: 32.2 us -> 30.2 us
    pallas_call x1, Pallas kernels: 32.2 us -> 30.2 us  [fused(): pl.pallas_call(functools.partial(kernel, wide, cap), out_shape=jax.ShapeD...]
where the time goes in v3:
time: 32.4 us; the launch traced here: 32.3 us
  Pallas kernels  30.2 us (93%)
  local copies, waits for them, and re-layouts  2.12 us (7%)
    pallas_call x1, Pallas kernels, fused(): pl.pallas_call(functools.partial(kernel, wide, cap), out_shape=jax.ShapeD...  30.2 us
    unnamed x5, local copies, waits for them, and re-layouts  2.12 us

profile of v3, /device:TPU:0, one launch (start us, length us, event | category | flops | bytes accessed | tf_op | source)
XLA Modules:
  0.0 32.3 jit_solution(10874315542729765726)
XLA Ops:
  0.0 0.0 copy-start.1
  0.0 0.7 %copy-done.1 = s32[128]{0:T(128)S(1)} copy-done((s32[128]{0:T(128)S(1)}, s32[128]{0:T(128)}, u32[]{:S(2)}) %copy-start.1) | copy-done | bytes 536
  0.7 0.0 copy-start
  0.7 0.9 %copy-done = bf16[128,1024]{1,0:T(8,128)(2,1)S(1)} copy-done((bf16[128,1024]{1,0:T(8,128)(2,1)S(1)}, bf16[128,1024]{1,0:T(8,128)(2,1)}, u32[]{:S(2)}) %copy-start) | copy-done | bytes 262168
  1.6 30.2 %shard_map.28 = f32[1,128]{1,0:T(1,128)S(1)} custom-call(bf16[128,1024]{1,0:T(8,128)(2,1)S(1)} %copy-done, s32[1,128]{1,0:T(1,128)S(1)} %bitcast.2), custom_call_target="tpu_custom_call" | custom-call | tf_op jit(solution)/shard_map/pallas_call | solution.py:248
  31.8 0.5 %copy.4 = f32[128]{0:T(128)} copy(f32[128]{0:T(128)S(1)} %bitcast.3) | data formatting | bytes 1024
Async XLA Ops:
  0.0 0.7 %copy-start.1 = (s32[128]{0:T(128)S(1)}, s32[128]{0:T(128)}, u32[]{:S(2)}) copy-start(s32[128]{0:T(128)} %param.3) | copy-start | bytes 1540
  0.7 0.9 %copy-start = (bf16[128,1024]{1,0:T(8,128)(2,1)S(1)}, bf16[128,1024]{1,0:T(8,128)(2,1)}, u32[]{:S(2)}) copy-start(bf16[128,1024]{1,0:T(8,128)(2,1)} %emb_hbm.1) | copy-start | bytes 786436

commit v4 on v3

--- a/solution.py
+++ b/solution.py
@@ -132,34 +132,37 @@
         beside[k].wait_recv()
         onward[k].wait_recv()
 
-    query_lane = lax.broadcasted_iota(jnp.int32, (1, group), 1)
-
-    def block(key_half, query_half):
-        first = key_half * (half * group)
+    def block(key_first, key_count, query_first, query_count):
+        lanes_here = query_count * cap
         queries = jnp.concatenate(
             [
-                keys[pl.ds(pl.multiple_of((query_half * half + q) * group + s * cap, cap), cap), :]
-                for q in range(half)
+                keys[pl.ds(pl.multiple_of((query_first + q) * group + s * cap, cap), cap), :]
+                for q in range(query_count)
             ],
             axis=0,
         )
         kinds = lax.broadcasted_iota(jnp.int32, (LABELS, group), 0).astype(jnp.float32) + 1.0
-        query_tag = labels[s, query_half * half, 1:2]
-        for q in range(1, half):
-            query_tag = jnp.maximum(query_tag, labels[s, query_half * half + q, 1:2])
-        query_kind = jnp.where(kinds == query_tag, 1.0, 0.0).astype(jnp.bfloat16)
+        query_kinds = []
+        for base in range(0, query_count, 4):
+            query_tag = labels[s, query_first + base, 1:2]
+            for q in range(1, 4):
+                query_tag = jnp.maximum(query_tag, labels[s, query_first + base + q, 1:2])
+            query_kinds.append(jnp.where(kinds == query_tag, 1.0, 0.0).astype(jnp.bfloat16))
+        query_kind = jnp.concatenate(query_kinds, axis=1)
+        query_lane = lax.broadcasted_iota(jnp.int32, (1, lanes_here), 1)
         query_place = (
-            query_half * (half * group)
-            + lax.div(query_lane, cap) * group + s * cap + lax.rem(query_lane, cap)
-        )
+            query_first * group + lax.div(query_lane, cap) * group + s * cap
+            + lax.rem(query_lane, cap)
+        )
+        first = key_first * group
         scores = raw_scores(
-            keys[pl.ds(pl.multiple_of(first, group), half * group), :], queries
-        )
-        nearest = jnp.full((1, group), -1.0, jnp.float32)
-        for q in range(half):
-            key_tag = labels[0, key_half * half + q, 0:1]
+            keys[pl.ds(pl.multiple_of(first, group), key_count * group), :], queries
+        )
+        nearest = jnp.full((1, lanes_here), -1.0, jnp.float32)
+        for q in range(key_count):
+            key_tag = labels[0, key_first + q, 0:1]
             for t in range(1, 4):
-                key_tag = jnp.maximum(key_tag, labels[t, key_half * half + q, 0:1])
+                key_tag = jnp.maximum(key_tag, labels[t, key_first + q, 0:1])
             key_kind = jnp.where(kinds == key_tag, 1.0, 0.0).astype(jnp.bfloat16)
             same = lax.dot_general(
                 key_kind, query_kind, (((0,), (0,)), ((), ())), preferred_element_type=jnp.float32
@@ -174,6 +177,7 @@
     pl.semaphore_wait(barrier, wide + 1)
     near_half = lax.div(w, half)
     far_half = 1 - near_half
+    pairs = [lax.div(peers[k], 2) * 2 for k in (4, 6)]
     for k in (4, 1, 2, 3, 5):
         routed[k].start()
     for k in others:
@@ -202,22 +206,26 @@
     tag_onward.wait_recv()
     for k in range(4):
         landed(k)
-    best[near_half] = block(near_half, near_half)
-    best[far_half] = jnp.full((1, group), -1.0, jnp.float32)
+    best[near_half] = block(near_half * half, half, near_half * half, half)
     routed[6].wait_recv()
     forward(6)
     relay(4)
     routed[7].wait_recv()
     forward(7)
-    for k in (5, 6, 7):
-        relay(k)
+    relay(5)
+    best[far_half] = block(near_half * half, half, far_half * half, half)
+    relay(6)
+    landed(4)
+    landed(5)
+    nearest = block(pairs[0], 2, 0, wide)
+    relay(7)
+    landed(6)
+    landed(7)
+    nearest = jnp.maximum(nearest, block(pairs[1], 2, 0, wide))
+    best[0] = jnp.maximum(best[0], nearest[:, :group])
+    best[1] = jnp.maximum(best[1], nearest[:, group:])
     for k in (1, 2, 3, 6, 7):
         routed[k].wait_send()
-    for k in range(4, 8):
-        landed(k)
-    across_best = block(0, 1)
-    best[far_half] = jnp.maximum(best[far_half], block(far_half, far_half))
-    best[1] = jnp.maximum(best[1], across_best)
     answers[w] = best[...]
     backs = [
         copy_to(best, answers.at[w], back_sems.at[0, k], back_sems.at[1, k], (peers[k], s))
@@ -248,7 +256,7 @@
     out = pl.pallas_call(
         functools.partial(kernel, wide, cap),
         out_shape=jax.ShapeDtypeStruct((1, docs), jnp.float32),
-        in_specs=[pl.BlockSpec(memory_space=pltpu.HBM)] * 2,
+        in_specs=[pl.BlockSpec(memory_space=pl.ANY)] * 2,
         out_specs=pl.BlockSpec(memory_space=pltpu.VMEM),
         scratch_shapes=[
             pltpu.VMEM((docs, width), jnp.bfloat16),
@@ -266,7 +274,7 @@
             pltpu.SemaphoreType.DMA((2, wide)),
         ],
         compiler_params=pltpu.CompilerParams(
-            collective_id=0, has_side_effects=True, vmem_limit_bytes=32 * 2**20
+            collective_id=0, has_side_effects=True
         ),
     )(embeddings, cluster_ids.reshape(1, docs))
     return out.reshape(docs)

time: 32.4 us -> 31.6 us (0.975)
  local copies, waits for them, and re-layouts: 2.12 us -> 1.1 us
    unnamed x5 -> x3, local copies, waits for them, and re-layouts: 2.12 us -> 1.1 us
where the time goes in v4:
time: 31.6 us; the launch traced here: 31.4 us
  Pallas kernels  30.3 us (96%)
  local copies, waits for them, and re-layouts  1.1 us (3%)
    pallas_call x1, Pallas kernels, fused(): pl.pallas_call(functools.partial(kernel, wide, cap), out_shape=jax.ShapeD...  30.3 us
    unnamed x3, local copies, waits for them, and re-layouts  1.1 us

profile of v4, /device:TPU:0, one launch (start us, length us, event | category | flops | bytes accessed | tf_op | source)
XLA Modules:
  0.0 31.4 jit_solution(4850364466192633401)
XLA Ops:
  0.0 30.3 %shard_map.28 = f32[1,128]{1,0:T(1,128)} custom-call(bf16[128,1024]{1,0:T(8,128)(2,1)} %emb_hbm.1, s32[1,128]{1,0:T(1,128)} %bitcast.2), custom_call_target="tpu_custom_call" | custom-call | tf_op jit(solution)/shard_map/pallas_call | solution.py:256
  30.3 0.0 copy-start
  30.3 0.6 %copy-done = f32[1,128]{1,0:T(1,128)S(1)} copy-done((f32[1,128]{1,0:T(1,128)S(1)}, f32[1,128]{1,0:T(1,128)}, u32[]{:S(2)}) %copy-start) | copy-done | bytes 536
  30.9 0.5 %copy.4 = f32[128]{0:T(128)} copy(f32[128]{0:T(128)S(1)} %bitcast.3) | data formatting | bytes 1024
Async XLA Ops:
  30.3 0.6 %copy-start = (f32[1,128]{1,0:T(1,128)S(1)}, f32[1,128]{1,0:T(1,128)}, u32[]{:S(2)}) copy-start(f32[1,128]{1,0:T(1,128)} %shard_map.28) | copy-start | bytes 1540
